TPU v7x, 128 devices: a whole 4x4x4 slice. The times are simulated.
128 devices in a mesh: row: 16 (over x, y_hi, core), col: 8 (over z, y_lo).
Axes of the slice: x: 4, y: 4 (y_hi: 2, y_lo: 2; y = y_hi * 2 + y_lo), z: 4, core: 2. Of those that a mesh axis runs over, the one named last changes fastest.
Arguments:
- features: bfloat16 [131072, 128], P(('row', 'col')), may hold values from -6 to 6
- weight: bfloat16 [128, 128], replicated, may hold values from -0.5 to 0.5
- layer_bias: float32 [128], replicated, may hold values from -3 to 3
- cotangent: bfloat16 [131072, 128], P(('col', 'row')), may hold values from -6 to 6
- tile_out: int32 [16, 8, 128], P('row', 'col'), may hold values from 0 to 63
- tile_in: int32 [16, 8, 128], P('row', 'col'), may hold values from 0 to 31
- tile_vals: bfloat16 [16, 8, 128, 256, 256], P('row', 'col'), may hold values from -0.09375 to 0.09375
- tile_count: int32 [16, 8], P('row', 'col'), may hold values from 1 to 128, as said below
Outputs:
- hidden_out: bfloat16 [131072, 128], P(('col', 'row'))
- feature_grad: bfloat16 [131072, 128], P(('row', 'col'))
- weight_grad: float32 [128, 128], replicated
- bias_grad: float32 [128], replicated
Inputs may be any that keep to these rules, and one draw needn't show every extreme that they name: `tile_count`: live slots of each grid block; some grid block has exactly 128 in every draw.
All inputs are finite; a program needn't handle non-finite values.
Results may differ from a plain program's by a relative error of at most 0.025.
Values may be sent and summed in bfloat16 or wider, within the bound.
No kernel may reach another device: no remote copies, remote signals or barrier semaphores. Data moves between devices by JAX's collectives and lax.ppermute only.
A program may use at most 192 MiB of HBM per device.

v0:
```python
import math
import jax
import jax.numpy as jnp
from jax import lax
from jax.sharding import PartitionSpec as P

gelu_coef = 0.7978845608
cube_coef = 0.044715


def gelu_tanh(inputs):
    inner = jnp.tanh(gelu_coef * (inputs + cube_coef * inputs * inputs * inputs))
    return 0.5 * inputs * (1.0 + inner)


def gelu_slope(inputs):
    inner = jnp.tanh(gelu_coef * (inputs + cube_coef * inputs * inputs * inputs))
    return 0.5 * (1.0 + inner) + 0.5 * inputs * (1.0 - inner * inner) * gelu_coef * (
        1.0 + 3.0 * cube_coef * inputs * inputs
    )


def tile_sums(products, targets, live_mask, target_tiles):
    masked = products * live_mask[:, None, None]
    summed = (
        jnp.zeros((target_tiles, products.shape[1], products.shape[2]), jnp.float32)
        .at[targets]
        .add(masked)
    )
    return summed.reshape(target_tiles * products.shape[1], products.shape[2])


def local(features, weight, layer_bias, cotangent, tile_out, tile_in, tile_vals, tile_count):
    tile_size = tile_vals.shape[-1]
    slot_count = tile_vals.shape[2]
    node_rows = features.shape[0]
    feat_count = features.shape[1]
    rows_axis = lax.axis_size("row")
    cols_axis = lax.axis_size("col")
    target_tiles = rows_axis * node_rows // tile_size
    source_tiles = cols_axis * node_rows // tile_size
    out_index = tile_out[0, 0]
    in_index = tile_in[0, 0]
    values = tile_vals[0, 0]
    live_mask = (jnp.arange(slot_count, dtype=jnp.int32) < tile_count[0, 0]).astype(jnp.float32)
    source_rows = lax.all_gather(features, "col", axis=0, tiled=True)
    picked = jnp.take(source_rows.reshape(source_tiles, tile_size, feat_count), in_index, axis=0)
    products = jnp.einsum("tab,tbf->taf", values, picked, preferred_element_type=jnp.float32)
    partial_value = tile_sums(products, out_index, live_mask, target_tiles).astype(jnp.bfloat16)
    own_agg = (
        lax.psum_scatter(partial_value, "row", scatter_dimension=0, tiled=True)
        .astype(jnp.float32)
        .astype(jnp.bfloat16)
    )
    preact = jnp.dot(own_agg, weight, preferred_element_type=jnp.float32) + layer_bias
    hidden_out = gelu_tanh(preact).astype(jnp.bfloat16)
    own_grad = (cotangent.astype(jnp.float32) * gelu_slope(preact)).astype(jnp.bfloat16)
    grad_local = jnp.dot(own_grad, weight.T, preferred_element_type=jnp.float32).astype(
        jnp.bfloat16
    )
    target_grad = lax.all_gather(grad_local, "row", axis=0, tiled=True)
    weight_local = lax.dot_general(
        own_agg, own_grad, (((0,), (0,)), ((), ())), preferred_element_type=jnp.float32
    )
    bias_local = jnp.sum(own_grad.astype(jnp.float32), axis=0)
    weight_total, bias_total = lax.psum((weight_local, bias_local), ("row", "col"))
    norm_scale = 1.0 / math.sqrt(node_rows * rows_axis * cols_axis)
    weight_grad = weight_total * norm_scale
    bias_grad = bias_total * norm_scale
    picked_grad = jnp.take(
        target_grad.reshape(target_tiles, tile_size, feat_count), out_index, axis=0
    )
    back_products = jnp.einsum(
        "tab,taf->tbf", values, picked_grad, preferred_element_type=jnp.float32
    )
    back_partial = tile_sums(back_products, in_index, live_mask, source_tiles).astype(jnp.bfloat16)
    feature_grad = (
        lax.psum_scatter(back_partial, "col", scatter_dimension=0, tiled=True)
        .astype(jnp.float32)
        .astype(jnp.bfloat16)
    )
    return (hidden_out, feature_grad, weight_grad, bias_grad)


def solution(mesh):
    in_specs = (
        P(("row", "col"), None),
        P(),
        P(),
        P(("col", "row"), None),
        P("row", "col", None),
        P("row", "col", None),
        P("row", "col", None, None, None),
        P("row", "col"),
    )
    out_specs = (P(("col", "row"), None), P(("row", "col"), None), P(), P())
    return jax.shard_map(local, mesh=mesh, in_specs=in_specs, out_specs=out_specs, check_vma=False)
```

profile of v0, /device:TPU:1, one launch (start us, length us, event | category | flops | bytes accessed | tf_op | source)
XLA Modules:
  0.0 496.3 jit_solution(11982166304795398902)
XLA Ops:
  7.2 0.7 all-gather.3.cloned.1.call-update
  8.6 0.7 fusion.22
  9.9 0.7 compare_convert_fusion
  10.6 54.4 %all-gather.3.cloned.1.call-done = bf16[8192,128]{1,0:T(8,128)(2,1)} async-done(((bf16[1024,128]{1,0:T(8,128)(2,1)}), bf16[8192,128]{1,0:T(8,128)(2,1)}) %all-gather.3.cloned.1.call-update) | async-done | bytes 2097168 | tf_op jit(solution)/shard_map/all_gather | solution.py:46
  65.0 8.2 %gather_fusion = bf16[128,256,128]{2,1,0:T(8,128)(2,1)} fusion(bf16[32,256,128]{2,1,0:T(8,128)(2,1)} %bitcast.37, s32[1024]{0:T(1024)S(1)} %pad_clamp_fusion.1), kind=kCustom, calls=%fused_computation | custom fusion | bytes 16777728 | tf_op jit(solution)/shard_map/jit(_take)/gather | solution.py:47
  73.2 17.5 %multiply_bitcast_fusion.1 = f32[128,256,128]{1,2,0:T(8,128)} fusion(bf16[1,1,128,256,256]{4,3,2,1,0:T(8,128)(2,1)} %param.14, f32[128]{0:T(128)S(1)} %get-tuple-element.7, bf16[128,256,128]{2,1,0:T(8,128)(2,1)} %gather_fusion, pred[128]{0:T(512)(128)(4,1)S(1)} %get-tuple-element.8), kind=kOutput, calls=%fused_computation.9 | convolution fusion | flops 2155872256 | bytes 41943680 | tf_op jit(solution)/shard_map/tab,tbf->taf/dot_general | solution.py:48
  90.7 17.4 %copy.15 = f32[128,256,128]{2,1,0:T(8,128)} copy(f32[128,256,128]{1,2,0:T(8,128)} %multiply_bitcast_fusion.1) | data formatting | bytes 33554432 | tf_op jit(solution)/shard_map/mul | solution.py:24
  108.1 4.2 broadcast_in_dim.29
  112.3 38.5 %scatter_fusion = f32[64,256,128]{2,1,0:T(8,128)} fusion(f32[64,256,128]{2,1,0:T(8,128)} %broadcast_in_dim.29, s32[128]{0:T(128)S(1)} %fusion.21, f32[128,256,128]{2,1,0:T(8,128)} %copy.15), kind=kCustom, calls=%fused_computation.2 | custom fusion | flops 4194304 | bytes 50332160 | tf_op jit(solution)/shard_map/scatter-add | solution.py:28
  150.8 6.1 %convert_element_type.39 = bf16[64,256,128]{2,1,0:T(8,128)(2,1)} convert(f32[64,256,128]{2,1,0:T(8,128)} %scatter_fusion) | non-fusion elementwise | flops 2097152 | bytes 12582912 | tf_op jit(solution)/shard_map/convert_element_type | solution.py:49
  157.0 78.4 %reduce-scatter.3.cloned.1.call-done = bf16[1024,128]{1,0:T(8,128)(2,1)} async-done(((bf16[16384,128]{1,0:T(8,128)(2,1)}), bf16[1024,128]{1,0:T(8,128)(2,1)}) %reduce-scatter.3.cloned.1.call-update) | async-done | bytes 262160 | tf_op jit(solution)/shard_map/reduce_scatter | solution.py:51
  235.4 2.2 convert_reduce_fusion
  237.6 0.9 convolution_convert_fusion
  238.7 1.9 fusion.26
  240.8 54.7 %all-gather.5.cloned.1.call-done = bf16[16384,128]{1,0:T(8,128)(2,1)} async-done(((bf16[1024,128]{1,0:T(8,128)(2,1)}), bf16[16384,128]{1,0:T(8,128)(2,1)}) %all-gather.5.cloned.1.call-update) | async-done | bytes 4194320 | tf_op jit(solution)/shard_map/all_gather | solution.py:61
  295.4 8.7 %gather_fusion.1 = bf16[128,256,128]{2,1,0:T(8,128)(2,1)} fusion(bf16[64,256,128]{2,1,0:T(8,128)(2,1)} %bitcast.38, s32[1024]{0:T(1024)S(1)} %pad_clamp_fusion), kind=kCustom, calls=%fused_computation.1 | custom fusion | bytes 16777728 | tf_op jit(solution)/shard_map/jit(_take)/gather | solution.py:70
  304.2 14.0 %multiply_bitcast_fusion = f32[128,256,128]{1,2,0:T(8,128)} fusion(bf16[1,1,128,256,256]{4,3,2,1,0:T(8,128)(2,1)} %param.14, bf16[128,256,128]{2,1,0:T(8,128)(2,1)} %gather_fusion.1, f32[128]{0:T(128)S(1)} %get-tuple-element.7, pred[128]{0:T(512)(128)(4,1)S(1)} %compare_and_fusion), kind=kOutput, calls=%fused_computation.8 | convolution fusion | flops 2155872256 | bytes 41943680 | tf_op jit(solution)/shard_map/tab,taf->tbf/dot_general | solution.py:73
  318.2 17.4 %copy.17 = f32[128,256,128]{2,1,0:T(8,128)} copy(f32[128,256,128]{1,2,0:T(8,128)} %multiply_bitcast_fusion) | data formatting | bytes 33554432 | tf_op jit(solution)/shard_map/mul | solution.py:24
  335.6 2.4 broadcast_in_dim.32
  338.0 37.9 %scatter_fusion.1 = f32[32,256,128]{2,1,0:T(8,128)} fusion(f32[32,256,128]{2,1,0:T(8,128)} %broadcast_in_dim.32, s32[128]{0:T(128)S(1)} %fusion.22, f32[128,256,128]{2,1,0:T(8,128)} %copy.17), kind=kCustom, calls=%fused_computation.3 | custom fusion | flops 4194304 | bytes 50332160 | tf_op jit(solution)/shard_map/scatter-add | solution.py:28
  376.0 3.9 convert_element_type.45
  379.9 64.8 %psum.15 = f32[128]{0:T(128)S(1)} all-reduce(f32[128]{0:T(128)S(1)} %get-tuple-element.4), channel_id=1, replica_groups=mesh['row'=16,'col'=8] {'row','col'}, use_global_device_ids=true, to_apply=%region_6.7 | all-reduce | flops 128 | bytes 1024 | tf_op jit(solution)/shard_map/psum | solution.py:66
  445.2 1.5 broadcast_multiply_fusion
  446.6 43.1 %reduce-scatter.5.cloned.1.call-done = bf16[1024,128]{1,0:T(8,128)(2,1)} async-done(((bf16[8192,128]{1,0:T(8,128)(2,1)}), bf16[1024,128]{1,0:T(8,128)(2,1)}) %reduce-scatter.5.cloned.1.call-update) | async-done | bytes 262160 | tf_op jit(solution)/shard_map/reduce_scatter | solution.py:78
  (25 shorter events, 1.7 us)
Async XLA Ops:
  7.2 228.2 %copy-start = (bf16[128,128]{1,0:T(8,128)(2,1)S(1)}, bf16[128,128]{1,0:T(8,128)(2,1)}, u32[]{:S(2)}) copy-start(bf16[128,128]{1,0:T(8,128)(2,1)} %param.9) | copy-start | bytes 98308
  7.2 57.8 %all-gather.3.cloned.1.call-start = ((), (), s32[]{:S(2)}) async-start(), calls=%async_computation.2 | async-start | bytes 2359296 | tf_op jit(solution)/shard_map/all_gather | solution.py:46
  7.9 227.5 %reduce-scatter.3.cloned.1.call-start = ((), (), s32[]{:S(2)}) async-start(), calls=%async_computation.3 | async-start | bytes 4456448 | tf_op jit(solution)/shard_map/reduce_scatter | solution.py:51
  150.8 84.6 %copy-start.2 = (bf16[1024,128]{1,0:T(8,128)(2,1)S(1)}, bf16[1024,128]{1,0:T(8,128)(2,1)}, u32[]{:S(2)}) copy-start(bf16[1024,128]{1,0:T(8,128)(2,1)} %param.11) | copy-start | bytes 786436
  150.8 84.6 %copy-start.3 = (f32[128]{0:T(128)S(1)}, f32[128]{0:T(128)}, u32[]{:S(2)}) copy-start(f32[128]{0:T(128)} %param.10) | copy-start | bytes 1540
  150.8 87.8 %copy-start.4 = (s32[1,1,128]{2,1,0:T(1,128)S(1)}, s32[1,1,128]{2,1,0:T(1,128)}, u32[]{:S(2)}) copy-start(s32[1,1,128]{2,1,0:T(1,128)} %param.12) | copy-start | bytes 1540
  156.9 138.5 %all-gather.5.cloned.1.call-start = ((), (), s32[]{:S(2)}) async-start(), calls=%async_computation.4 | async-start | bytes 4456448 | tf_op jit(solution)/shard_map/all_gather | solution.py:61
  238.6 206.6 %all-reduce.2.cloned.1.call-start = ((), (), s32[]{:S(2)}) async-start(), calls=%async_computation.6 | async-start | bytes 131072 | tf_op jit(solution)/shard_map/psum | solution.py:66
  240.5 249.3 %reduce-scatter.5.cloned.1.call-start = ((), (), s32[]{:S(2)}) async-start(), calls=%async_computation.5 | async-start | bytes 2359296 | tf_op jit(solution)/shard_map/reduce_scatter | solution.py:78
  338.0 151.8 %copy-start.1 = (bf16[128,128]{1,0:T(8,128)(2,1)S(1)}, bf16[128,128]{1,0:T(8,128)(2,1)}, u32[]{:S(2)}) copy-start(bf16[128,128]{1,0:T(8,128)(2,1)} %param.9) | copy-start | bytes 98308
Sparse Core Ops, SparseCore 0:
  9.7 55.3 all-gather.2
  157.0 78.2 reduce-scatter.2
  238.7 56.6 all-gather.4
  301.3 136.4 all-reduce.1
  440.6 49.1 reduce-scatter.4
where the time goes:
time: 497 us; the launch traced here: 496 us
  waiting for transfers between devices  231 us (46%)
  other arithmetic  90.4 us (18%)
  blocking collectives  64.8 us (13%)
  local copies, waits for them, and re-layouts  58.4 us (12%)
  matrix products  36.6 us (7%)
  between operations  14.5 us (3%)
    reduce_scatter x1, waiting for transfers between devices, local(): lax.psum_scatter(partial_value, 'row', scatter_dimension=0, tiled=True)  78.4 us
    scatter-add x2, other arithmetic, tile_sums(): summed = jnp.zeros((target_tiles, products.shape[1], products.shape[2]),...  76.4 us
    psum x1, blocking collectives, local(): lax.psum((weight_local, bias_local), ('row', 'col'))  64.8 us
    all_gather x1, waiting for transfers between devices, local(): target_grad = lax.all_gather(grad_local, 'row', axis=0, tiled=True)  54.7 us
    all_gather x1, waiting for transfers between devices, local(): source_rows = lax.all_gather(features, 'col', axis=0, tiled=True)  54.4 us
    reduce_scatter x1, waiting for transfers between devices, local(): lax.psum_scatter(back_partial, 'col', scatter_dimension=0, tiled=True)  43.1 us
    mul x2, local copies, waits for them, and re-layouts, tile_sums(): masked = products * live_mask[:, None, None]  34.8 us
    dot_general x1, matrix products, local(): jnp.einsum('tab,tbf->taf', values, picked, preferred_element_type=jnp.flo...  17.5 us
  transfers between devices with their start and end apart: 5, of which 4 were waited for; matrix products, arithmetic and copies ran while one was open for 18% of the time, Pallas kernels for 0%

commit v1 on v0

--- a/solution.py
+++ b/solution.py
@@ -6,6 +6,15 @@
 
 gelu_coef = 0.7978845608
 cube_coef = 0.044715
+_search_run = lambda in_array, axis_key: jnp.concatenate(
+    lax.all_to_all(
+        jnp.stack([in_array] * lax.axis_size(axis_key)),
+        axis_name=axis_key,
+        split_axis=0,
+        concat_axis=0,
+    ),
+    axis=0,
+)
 
 
 def gelu_tanh(inputs):
@@ -43,7 +52,7 @@
     in_index = tile_in[0, 0]
     values = tile_vals[0, 0]
     live_mask = (jnp.arange(slot_count, dtype=jnp.int32) < tile_count[0, 0]).astype(jnp.float32)
-    source_rows = lax.all_gather(features, "col", axis=0, tiled=True)
+    source_rows = _search_run(features, "col")
     picked = jnp.take(source_rows.reshape(source_tiles, tile_size, feat_count), in_index, axis=0)
     products = jnp.einsum("tab,tbf->taf", values, picked, preferred_element_type=jnp.float32)
     partial_value = tile_sums(products, out_index, live_mask, target_tiles).astype(jnp.bfloat16)

time: 497 us -> 475 us (0.956)
  waiting for transfers between devices: 231 us -> 201 us
  starting transfers between devices: 0.38 us -> 7.22 us
    all_gather x1 -> x0, waiting for transfers between devices: 54.4 us -> none  [local(): source_rows = lax.all_gather(features, 'col', axis=0, tiled=True)]
    all_to_all x0 -> x1, waiting for transfers between devices: none -> 23.4 us  [lax.all_to_all(jnp.stack([in_array] * lax.axis_size(axis_key)), axis_name...]
    all_to_all x0 -> x1, starting transfers between devices: none -> 6.88 us  [lax.all_to_all(jnp.stack([in_array] * lax.axis_size(axis_key)), axis_name...]
  transfers between devices with their start and end apart: 5 -> 5, of which waited for: 4 -> 4; matrix products, arithmetic and copies ran while one was open for 18% -> 19% of each run, Pallas kernels for 0% -> 0%
where the time goes in v1:
time: 475 us; the launch traced here: 474 us
  waiting for transfers between devices  201 us (42%)
  other arithmetic  90.4 us (19%)
  blocking collectives  64.8 us (14%)
  local copies, waits for them, and re-layouts  59.4 us (13%)
  matrix products  36.6 us (8%)
  between operations  14.5 us (3%)
  starting transfers between devices  7.22 us (2%)
    reduce_scatter x1, waiting for transfers between devices, local(): lax.psum_scatter(partial_value, 'row', scatter_dimension=0, tiled=True)  80 us
    scatter-add x2, other arithmetic, tile_sums(): summed = jnp.zeros((target_tiles, products.shape[1], products.shape[2]),...  76.4 us
    psum x1, blocking collectives, local(): lax.psum((weight_local, bias_local), ('row', 'col'))  64.8 us
    all_gather x1, waiting for transfers between devices, local(): target_grad = lax.all_gather(grad_local, 'row', axis=0, tiled=True)  54.7 us
    reduce_scatter x1, waiting for transfers between devices, local(): lax.psum_scatter(back_partial, 'col', scatter_dimension=0, tiled=True)  43.3 us
    mul x2, local copies, waits for them, and re-layouts, tile_sums(): masked = products * live_mask[:, None, None]  34.8 us
    all_to_all x1, waiting for transfers between devices, lax.all_to_all(jnp.stack([in_array] * lax.axis_size(axis_key)), axis_name...  23.4 us
    dot_general x1, matrix products, local(): jnp.einsum('tab,tbf->taf', values, picked, preferred_element_type=jnp.flo...  17.5 us
  transfers between devices with their start and end apart: 5, of which 4 were waited for; matrix products, arithmetic and copies ran while one was open for 19% of the time, Pallas kernels for 0%

profile of v1, /device:TPU:1, one launch (start us, length us, event | category | flops | bytes accessed | tf_op | source)
XLA Modules:
  0.0 474.2 jit_solution(1333036969258003019)
XLA Ops:
  7.2 2.6 stack.2
  9.8 6.9 %all-to-all-start = ((bf16[8,1024,128]{2,1,0:T(8,128)(2,1)}), bf16[8,1024,128]{2,1,0:T(8,128)(2,1)S(1)}, u32[]{:S(2)}, u32[]{:S(2)}) async-start(bf16[8,1024,128]{2,1,0:T(8,128)(2,1)} %stack.2), calls=%async_computation | async-start | bytes 4194304 | tf_op jit(solution)/shard_map/all_to_all | solution.py:10
  18.6 0.7 compare_convert_fusion
  19.3 23.4 %all-to-all-done = bf16[8,1024,128]{2,1,0:T(8,128)(2,1)S(1)} async-done(((bf16[8,1024,128]{2,1,0:T(8,128)(2,1)}), bf16[8,1024,128]{2,1,0:T(8,128)(2,1)S(1)}, u32[]{:S(2)}, u32[]{:S(2)}) %all-to-all-start) | async-done | bytes 2097184 | tf_op jit(solution)/shard_map/all_to_all | solution.py:10
  42.7 6.6 %gather_fusion = bf16[128,256,128]{2,1,0:T(8,128)(2,1)} fusion(bf16[32,256,128]{2,1,0:T(8,128)(2,1)S(1)} %bitcast.37, s32[1024]{0:T(1024)S(1)} %pad_clamp_fusion.1), kind=kCustom, calls=%fused_computation | custom fusion | bytes 16777728 | tf_op jit(solution)/shard_map/jit(_take)/gather | solution.py:56
  49.3 17.5 %multiply_bitcast_fusion.1 = f32[128,256,128]{1,2,0:T(8,128)} fusion(bf16[1,1,128,256,256]{4,3,2,1,0:T(8,128)(2,1)} %param.14, f32[128]{0:T(128)S(1)} %get-tuple-element.7, bf16[128,256,128]{2,1,0:T(8,128)(2,1)} %gather_fusion, pred[128]{0:T(512)(128)(4,1)S(1)} %get-tuple-element.8), kind=kOutput, calls=%fused_computation.9 | convolution fusion | flops 2155872256 | bytes 41943680 | tf_op jit(solution)/shard_map/tab,tbf->taf/dot_general | solution.py:57
  66.8 17.4 %copy.15 = f32[128,256,128]{2,1,0:T(8,128)} copy(f32[128,256,128]{1,2,0:T(8,128)} %multiply_bitcast_fusion.1) | data formatting | bytes 33554432 | tf_op jit(solution)/shard_map/mul | solution.py:33
  84.2 4.2 broadcast_in_dim.29
  88.4 38.5 %scatter_fusion = f32[64,256,128]{2,1,0:T(8,128)} fusion(f32[64,256,128]{2,1,0:T(8,128)} %broadcast_in_dim.29, s32[128]{0:T(128)S(1)} %fusion.21, f32[128,256,128]{2,1,0:T(8,128)} %copy.15), kind=kCustom, calls=%fused_computation.2 | custom fusion | flops 4194304 | bytes 50332160 | tf_op jit(solution)/shard_map/scatter-add | solution.py:37
  126.9 6.1 %convert_element_type.39 = bf16[64,256,128]{2,1,0:T(8,128)(2,1)} convert(f32[64,256,128]{2,1,0:T(8,128)} %scatter_fusion) | non-fusion elementwise | flops 2097152 | bytes 12582912 | tf_op jit(solution)/shard_map/convert_element_type | solution.py:58
  133.1 80.0 %reduce-scatter.3.cloned.1.call-done = bf16[1024,128]{1,0:T(8,128)(2,1)} async-done(((bf16[16384,128]{1,0:T(8,128)(2,1)}), bf16[1024,128]{1,0:T(8,128)(2,1)}) %reduce-scatter.3.cloned.1.call-update) | async-done | bytes 262160 | tf_op jit(solution)/shard_map/reduce_scatter | solution.py:60
  213.1 2.2 convert_reduce_fusion
  215.3 0.9 convolution_convert_fusion
  216.3 1.9 fusion.26
  218.4 54.7 %all-gather.2.cloned.1.call-done = bf16[16384,128]{1,0:T(8,128)(2,1)} async-done(((bf16[1024,128]{1,0:T(8,128)(2,1)}), bf16[16384,128]{1,0:T(8,128)(2,1)}) %all-gather.2.cloned.1.call-update) | async-done | bytes 4194320 | tf_op jit(solution)/shard_map/all_gather | solution.py:70
  273.1 8.8 %gather_fusion.1 = bf16[128,256,128]{2,1,0:T(8,128)(2,1)} fusion(bf16[64,256,128]{2,1,0:T(8,128)(2,1)} %bitcast.38, s32[1024]{0:T(1024)S(1)} %pad_clamp_fusion), kind=kCustom, calls=%fused_computation.1 | custom fusion | bytes 16777728 | tf_op jit(solution)/shard_map/jit(_take)/gather | solution.py:79
  281.9 14.0 %multiply_bitcast_fusion = f32[128,256,128]{1,2,0:T(8,128)} fusion(bf16[1,1,128,256,256]{4,3,2,1,0:T(8,128)(2,1)} %param.14, bf16[128,256,128]{2,1,0:T(8,128)(2,1)} %gather_fusion.1, f32[128]{0:T(128)S(1)} %get-tuple-element.7, pred[128]{0:T(512)(128)(4,1)S(1)} %compare_and_fusion), kind=kOutput, calls=%fused_computation.8 | convolution fusion | flops 2155872256 | bytes 41943680 | tf_op jit(solution)/shard_map/tab,taf->tbf/dot_general | solution.py:82
  295.9 17.4 %copy.17 = f32[128,256,128]{2,1,0:T(8,128)} copy(f32[128,256,128]{1,2,0:T(8,128)} %multiply_bitcast_fusion) | data formatting | bytes 33554432 | tf_op jit(solution)/shard_map/mul | solution.py:33
  313.3 2.4 broadcast_in_dim.32
  315.8 37.9 %scatter_fusion.1 = f32[32,256,128]{2,1,0:T(8,128)} fusion(f32[32,256,128]{2,1,0:T(8,128)} %broadcast_in_dim.32, s32[128]{0:T(128)S(1)} %fusion.22, f32[128,256,128]{2,1,0:T(8,128)} %copy.17), kind=kCustom, calls=%fused_computation.3 | custom fusion | flops 4194304 | bytes 50332160 | tf_op jit(solution)/shard_map/scatter-add | solution.py:37
  353.7 3.9 convert_element_type.45
  357.6 64.8 %psum.15 = f32[128]{0:T(128)S(1)} all-reduce(f32[128]{0:T(128)S(1)} %get-tuple-element.4), channel_id=1, replica_groups=mesh['row'=16,'col'=8] {'row','col'}, use_global_device_ids=true, to_apply=%region_6.7 | all-reduce | flops 128 | bytes 1024 | tf_op jit(solution)/shard_map/psum | solution.py:75
  422.9 1.5 broadcast_multiply_fusion
  424.4 43.3 %reduce-scatter.5.cloned.1.call-done = bf16[1024,128]{1,0:T(8,128)(2,1)} async-done(((bf16[8192,128]{1,0:T(8,128)(2,1)}), bf16[1024,128]{1,0:T(8,128)(2,1)}) %reduce-scatter.5.cloned.1.call-update) | async-done | bytes 262160 | tf_op jit(solution)/shard_map/reduce_scatter | solution.py:87
  (25 shorter events, 2.3 us)
Async XLA Ops:
  7.2 205.9 %copy-start = (bf16[128,128]{1,0:T(8,128)(2,1)S(1)}, bf16[128,128]{1,0:T(8,128)(2,1)}, u32[]{:S(2)}) copy-start(bf16[128,128]{1,0:T(8,128)(2,1)} %param.9) | copy-start | bytes 98308
  9.8 32.9 %all-to-all-start = ((bf16[8,1024,128]{2,1,0:T(8,128)(2,1)}), bf16[8,1024,128]{2,1,0:T(8,128)(2,1)S(1)}, u32[]{:S(2)}, u32[]{:S(2)}) async-start(bf16[8,1024,128]{2,1,0:T(8,128)(2,1)} %stack.2), calls=%async_computation | async-start | bytes 4194304 | tf_op jit(solution)/shard_map/all_to_all | solution.py:10
  16.6 196.4 %reduce-scatter.3.cloned.1.call-start = ((), (), s32[]{:S(2)}) async-start(), calls=%async_computation.3 | async-start | bytes 4456448 | tf_op jit(solution)/shard_map/reduce_scatter | solution.py:60
  126.9 86.2 %copy-start.2 = (bf16[1024,128]{1,0:T(8,128)(2,1)S(1)}, bf16[1024,128]{1,0:T(8,128)(2,1)}, u32[]{:S(2)}) copy-start(bf16[1024,128]{1,0:T(8,128)(2,1)} %param.11) | copy-start | bytes 786436
  126.9 86.2 %copy-start.3 = (f32[128]{0:T(128)S(1)}, f32[128]{0:T(128)}, u32[]{:S(2)}) copy-start(f32[128]{0:T(128)} %param.10) | copy-start | bytes 1540
  126.9 89.4 %copy-start.4 = (s32[1,1,128]{2,1,0:T(1,128)S(1)}, s32[1,1,128]{2,1,0:T(1,128)}, u32[]{:S(2)}) copy-start(s32[1,1,128]{2,1,0:T(1,128)} %param.12) | copy-start | bytes 1540
  133.0 140.1 %all-gather.2.cloned.1.call-start = ((), (), s32[]{:S(2)}) async-start(), calls=%async_computation.4 | async-start | bytes 4456448 | tf_op jit(solution)/shard_map/all_gather | solution.py:70
  216.2 206.6 %all-reduce.2.cloned.1.call-start = ((), (), s32[]{:S(2)}) async-start(), calls=%async_computation.6 | async-start | bytes 131072 | tf_op jit(solution)/shard_map/psum | solution.py:75
  218.2 249.5 %reduce-scatter.5.cloned.1.call-start = ((), (), s32[]{:S(2)}) async-start(), calls=%async_computation.5 | async-start | bytes 2359296 | tf_op jit(solution)/shard_map/reduce_scatter | solution.py:87
  315.8 151.9 %copy-start.1 = (bf16[128,128]{1,0:T(8,128)(2,1)S(1)}, bf16[128,128]{1,0:T(8,128)(2,1)}, u32[]{:S(2)}) copy-start(bf16[128,128]{1,0:T(8,128)(2,1)} %param.9) | copy-start | bytes 98308
Sparse Core Ops, SparseCore 0:
  133.2 79.8 reduce-scatter.2
  216.4 56.7 all-gather.1
  279.2 136.4 all-reduce.1
  418.5 49.1 reduce-scatter.4
